TPU v7x, 32 devices: a whole 2x2x4 slice. The times are simulated.
32 devices in a mesh: tm: 16 (over z, y, x), row: 2 (over core).
Axes of the slice: x: 2, y: 2, z: 4, core: 2. Of those that a mesh axis runs over, the one named last changes fastest.
Arguments:
- transition: float32 [1024, 1024], P('row'), may hold values from -1 to 1, as said below
- gain_fwd: float32 [1024, 1024], P(None, 'row'), may hold values from -0.0234375 to 0.0234375
- gain_bwd: float32 [1024, 1024], P(None, 'row'), may hold values from -0.0234375 to 0.0234375
- blend: float32 [1024, 1024], P(None, 'row'), may hold values from -0.1875 to 0.1875
- prior_state: float32 [1024], replicated, may hold values from -6 to 6
- final_state: float32 [1024], replicated, may hold values from -6 to 6
- obs_index: int32 [512, 128], P('tm'), may hold values from 0 to 1023
- obs_visible: int32 [512, 128], P('tm'), may hold values 0 or 1
- obs_value: float32 [512, 128], P('tm'), may hold values from -6 to 6
Outputs:
- smoothed: float32 [512, 1024], P('tm', 'row')
Inputs may be any that keep to these rules, and one draw needn't show every extreme that they name: `transition`: symmetric; every eigenvalue lies strictly between 0 and 1.
All inputs are finite; a program needn't handle non-finite values. No bound on the sum of `obs_visible` on one device may be relied on, other than what follows from the above.
Results may differ from a plain program's by a relative error of at most 0.0003.
Values sent between devices are 32-bit elements; how exact they have to be, the bound alone decides.
A program may use at most 128 MiB of HBM per device.

v0:
```python
import jax
import jax.numpy as jnp
from jax import lax
from jax.sharding import PartitionSpec as P


def passed_along(array, axis, by):
    length = lax.axis_size(axis)
    pairs = [(i, i + by) for i in range(length) if 0 <= i + by < length]
    return lax.ppermute(array, axis, pairs)


def square_slab(slab_rows):

    def accumulate(total, block_rows, first_row):
        return jnp.dot(slab_rows, block_rows, precision=lax.Precision.HIGHEST)

    return accumulate(
        jnp.zeros_like(slab_rows),
        lax.all_gather(slab_rows, "row", axis=0, tiled=True),
        jnp.int32(0),
    )


def square_level(slab_rows):

    def accumulate(total, block_rows, first_row):
        return jnp.dot(slab_rows, block_rows, precision=lax.Precision.HIGHEST)

    return accumulate(
        jnp.zeros_like(slab_rows),
        lax.all_gather(slab_rows, "row", axis=0, tiled=True),
        jnp.int32(0),
    )


def ladder_slabs(slab_rows, full_matrix, levels):
    slab_list = [slab_rows]
    full_list = [full_matrix]
    for level in range(1, levels + 1):
        squared = square_slab(slab_list[-1])
        slab_list.append(squared)
        if level < levels:
            full_list.append(lax.all_gather(squared, "row", axis=0, tiled=True))
    return (full_list, slab_list[levels])


def sweep(full_list, innov_fwd, innov_bwd, start_fwd, start_bwd):
    epochs = innov_fwd.shape[0]
    state_size = innov_fwd.shape[1]
    contract = (((1,), (1,)), ((), ()))
    starts = jnp.stack((start_fwd, start_bwd), axis=0)
    heads = lax.dot_general(starts, full_list[0], contract, precision=lax.Precision.HIGHEST)
    paired = jnp.stack((innov_fwd, innov_bwd[::-1]), axis=0)
    paired = paired.at[:, 0, :].add(heads)
    for level, power in enumerate(full_list):
        step_size = 1 << level
        shifted = jnp.concatenate(
            (
                jnp.zeros((2, step_size, state_size), jnp.float32),
                paired[:, : epochs - step_size, :],
            ),
            axis=1,
        )
        paired = paired + lax.dot_general(
            shifted, power, (((2,), (1,)), ((), ())), precision=lax.Precision.HIGHEST
        )
    seq_fwd = paired[0]
    seq_bwd = paired[1][::-1]
    return (seq_fwd[-1], seq_bwd[0], seq_fwd, seq_bwd)


def per_device(
    transition,
    gain_fwd,
    gain_bwd,
    blend,
    prior_state,
    final_state,
    obs_index,
    obs_visible,
    obs_value,
):
    highest = lax.Precision.HIGHEST
    slab_count = transition.shape[0]
    state_size = transition.shape[1]
    epochs = obs_index.shape[0]
    levels = (epochs - 1).bit_length()
    offset = lax.axis_index("row") * slab_count
    weights = obs_value * obs_visible.astype(jnp.float32)
    places = jnp.broadcast_to(jnp.arange(epochs, dtype=jnp.int32)[:, None], obs_index.shape)
    sparse = jnp.zeros((epochs, state_size), jnp.float32).at[places, obs_index].add(weights)
    fwd_part = jnp.dot(sparse, gain_fwd, precision=highest)
    bwd_part = jnp.dot(sparse, gain_bwd, precision=highest)
    innov_fwd, innov_bwd = (
        lax.all_gather(fwd_part, "row", axis=1, tiled=True),
        lax.all_gather(bwd_part, "row", axis=1, tiled=True),
    )
    full_matrix = lax.all_gather(transition, "row", axis=0, tiled=True)
    full_list, segment_map = ladder_slabs(transition, full_matrix, levels)
    segment_index = lax.axis_index("tm")
    segments = lax.axis_size("tm")
    nothing = jnp.zeros((state_size,), jnp.float32)
    head_fwd = jnp.where(segment_index == 0, prior_state, nothing)
    head_bwd = jnp.where(segment_index == segments - 1, final_state, nothing)
    offset_fwd, offset_bwd, _, _ = sweep(full_list, innov_fwd, innov_bwd, head_fwd, head_bwd)
    enter_fwd = passed_along(offset_fwd, "tm", 1)
    enter_bwd = passed_along(offset_bwd, "tm", -1)
    level_map = segment_map
    for section_index in range((segments - 1).bit_length()):
        if section_index > 0:
            level_map = square_level(level_map)
        received_fwd = passed_along(enter_fwd, "tm", 1 << section_index)
        received_bwd = passed_along(enter_bwd, "tm", -(1 << section_index))
        added_fwd = jnp.dot(level_map, received_fwd, precision=highest)
        added_bwd = jnp.dot(level_map, received_bwd, precision=highest)
        full_fwd, full_bwd = (
            lax.all_gather(added_fwd, "row", axis=0, tiled=True),
            lax.all_gather(added_bwd, "row", axis=0, tiled=True),
        )
        enter_fwd = enter_fwd + full_fwd
        enter_bwd = enter_bwd + full_bwd
    start_fwd = enter_fwd + head_fwd
    start_bwd = enter_bwd + head_bwd
    _, _, seq_fwd, seq_bwd = sweep(full_list, innov_fwd, innov_bwd, start_fwd, start_bwd)
    own_states = lax.dynamic_slice_in_dim(seq_fwd, offset, slab_count, 1)
    return own_states + jnp.dot(seq_bwd - seq_fwd, blend, precision=highest)


def solution(mesh):
    placed = (
        P("row", None),
        P(None, "row"),
        P(None, "row"),
        P(None, "row"),
        P(),
        P(),
        P("tm", None),
        P("tm", None),
        P("tm", None),
    )
    return jax.shard_map(
        per_device, mesh=mesh, in_specs=placed, out_specs=P("tm", "row"), check_vma=False
    )
```

profile of v0, /device:TPU:7, one launch (start us, length us, event | category | flops | bytes accessed | tf_op | source)
XLA Modules:
  0.0 353.6 jit_solution(17095813674647343786)
XLA Ops:
  7.3 17.2 %all-gather.17.cloned.1.call-done = f32[1024,1024]{1,0:T(8,128)} async-done(((f32[512,1024]{1,0:T(8,128)}), f32[1024,1024]{1,0:T(8,128)}) %all-gather.17.cloned.1.call-update) | async-done | bytes 4194320 | tf_op jit(solution)/shard_map/all_gather | solution.py:99
  24.5 10.3 %fusion.89 = f32[512,1024]{1,0:T(8,128)} fusion(f32[512,1024]{1,0:T(8,128)} %param.13, f32[1024,1024]{1,0:T(8,128)} %all-gather.17.cloned.1.call-done), kind=kOutput, calls=%fused_computation.95 | convolution fusion | flops 6442450944 | bytes 8388608 | tf_op jit(solution)/shard_map/dot_general | solution.py:16
  34.8 14.9 %all-gather.19.cloned.1.call-done = f32[1024,1024]{1,0:T(8,128)} async-done(((f32[512,1024]{1,0:T(8,128)}), f32[1024,1024]{1,0:T(8,128)}) %all-gather.19.cloned.1.call-update) | async-done | bytes 4194320 | tf_op jit(solution)/shard_map/all_gather | solution.py:44
  49.8 10.2 %fusion.90 = f32[512,1024]{1,0:T(8,128)} fusion(f32[512,1024]{1,0:T(8,128)} %fusion.89, f32[1024,1024]{1,0:T(8,128)} %all-gather.19.cloned.1.call-done), kind=kOutput, calls=%fused_computation.96 | convolution fusion | flops 6442450944 | bytes 8388608 | tf_op jit(solution)/shard_map/dot_general | solution.py:16
  60.1 14.9 %all-gather.21.cloned.1.call-done = f32[1024,1024]{1,0:T(8,128)} async-done(((f32[512,1024]{1,0:T(8,128)}), f32[1024,1024]{1,0:T(8,128)}) %all-gather.21.cloned.1.call-update) | async-done | bytes 4194320 | tf_op jit(solution)/shard_map/all_gather | solution.py:44
  75.0 10.3 %fusion.91 = f32[512,1024]{1,0:T(8,128)} fusion(f32[512,1024]{1,0:T(8,128)} %fusion.90, f32[1024,1024]{1,0:T(8,128)} %all-gather.21.cloned.1.call-done), kind=kOutput, calls=%fused_computation.97 | convolution fusion | flops 6442450944 | bytes 8388608 | tf_op jit(solution)/shard_map/dot_general | solution.py:16
  85.6 14.8 %all-gather.23.cloned.1.call-done = f32[1024,1024]{1,0:T(8,128)} async-done(((f32[512,1024]{1,0:T(8,128)}), f32[1024,1024]{1,0:T(8,128)}) %all-gather.23.cloned.1.call-update) | async-done | bytes 4194320 | tf_op jit(solution)/shard_map/all_gather | solution.py:44
  100.3 10.3 %fusion.92 = f32[512,1024]{1,0:T(8,128)} fusion(f32[512,1024]{1,0:T(8,128)} %fusion.91, f32[1024,1024]{1,0:T(8,128)} %all-gather.23.cloned.1.call-done), kind=kOutput, calls=%fused_computation.98 | convolution fusion | flops 6442450944 | bytes 8388608 | tf_op jit(solution)/shard_map/dot_general | solution.py:16
  110.7 14.9 %all-gather.25.cloned.1.call-done = f32[1024,1024]{1,0:T(8,128)} async-done(((f32[512,1024]{1,0:T(8,128)}), f32[1024,1024]{1,0:T(8,128)}) %all-gather.25.cloned.1.call-update) | async-done | bytes 4194320 | tf_op jit(solution)/shard_map/all_gather | solution.py:44
  125.6 10.3 %fusion.93 = f32[512,1024]{1,0:T(8,128)} fusion(f32[512,1024]{1,0:T(8,128)} %fusion.92, f32[1024,1024]{1,0:T(8,128)} %all-gather.25.cloned.1.call-done), kind=kOutput, calls=%fused_computation.99 | convolution fusion | flops 6442450944 | bytes 8388608 | tf_op jit(solution)/shard_map/dot_general | solution.py:16
  135.9 14.9 %all-gather.27.cloned.1.call-done = f32[1024,1024]{1,0:T(8,128)} async-done(((f32[512,1024]{1,0:T(8,128)}), f32[1024,1024]{1,0:T(8,128)}) %all-gather.27.cloned.1.call-update) | async-done | bytes 4194320 | tf_op jit(solution)/shard_map/all_gather | solution.py:32
  150.9 10.3 %fusion.94 = f32[512,1024]{1,0:T(8,128)} fusion(f32[512,1024]{1,0:T(8,128)} %fusion.93, f32[1024,1024]{1,0:T(8,128)} %all-gather.27.cloned.1.call-done), kind=kOutput, calls=%fused_computation.100 | convolution fusion | flops 6442450944 | bytes 8388608 | tf_op jit(solution)/shard_map/dot_general | solution.py:28
  162.1 29.0 %scatter_custom_fusion = f32[32768]{0:T(1024)S(1)} fusion(s32[4096]{0:T(1024)S(1)} %select_bitcast_fusion, f32[4096]{0:T(1024)S(1)} %multiply_bitcast_fusion, f32[]{:T(128)} %constant.67.clone.1), kind=kCustom, calls=%fused_computation.55 | custom fusion | flops 4096 | bytes 131076
  192.5 10.3 %fusion.95 = f32[512,1024]{1,0:T(8,128)} fusion(f32[512,1024]{1,0:T(8,128)} %fusion.94, f32[1024,1024]{1,0:T(8,128)} %all-gather.29.cloned.1.call-done), kind=kOutput, calls=%fused_computation.101 | convolution fusion | flops 6442450944 | bytes 8388608 | tf_op jit(solution)/shard_map/dot_general | solution.py:28
  209.7 6.2 %fusion.64 = f32[2,1024]{1,0:T(2,128)S(1)} fusion(f32[1024,1024]{1,0:T(8,128)} %all-gather.17.cloned.1.call-done, f32[1,1024]{1,0:T(1,128)S(1)} %bitcast.177, f32[1,1024]{1,0:T(1,128)S(1)} %bitcast.178), kind=kOutput, calls=%fused_computation.65 | convolution fusion | flops 25167872 | bytes 4210688 | tf_op jit(solution)/shard_map/dot_general | solution.py:53
  216.5 6.4 %fusion.20 = f32[2,32,1024]{2,1,0:T(8,128)S(1)} fusion(f32[2,32,1024]{2,1,0:T(8,128)S(1)} %scatter-add.18, f32[1024,1024]{1,0:T(8,128)} %all-gather.17.cloned.1.call-done, f32[2,31,1024]{2,1,0:T(8,128)S(1)} %bitcast.159), kind=kOutput, calls=%fused_computation.21 | convolution fusion | flops 805371904 | bytes 4972544 | tf_op jit(solution)/shard_map/dot_general | solution.py:65
  231.3 4.3 %fusion.38 = f32[2,32,1024]{2,1,0:T(8,128)S(1)} fusion(f32[2,32,1024]{2,1,0:T(8,128)S(1)} %fusion.32, f32[1024,1024]{1,0:T(8,128)S(1)} %copy-done.9, f32[2,24,1024]{2,1,0:T(8,128)S(1)} %slice.110), kind=kOutput, calls=%fused_computation.27 | convolution fusion | flops 805371904 | bytes 4915200 | tf_op jit(solution)/shard_map/dot_general | solution.py:65
  241.9 4.9 %collective-permute-start = (f32[1024]{0:T(1024)S(1)}, f32[1024]{0:T(1024)S(1)}, u32[]{:S(2)}, u32[]{:S(2)}) collective-permute-start(f32[1024]{0:T(1024)S(1)} %bitcast.189), channel_id=1, source_target_pairs={{0,2},{2,4},{4,6},{6,8},{8,10},{10,12},{12,14},{14,16},{16,18},{18... | collective-permute-start | bytes 12296 | tf_op jit(solution)/shard_map/ppermute | solution.py:10
  248.8 5.3 %collective-permute-start.1 = (f32[1024]{0:T(1024)S(1)}, f32[1024]{0:T(1024)S(1)}, u32[]{:S(2)}, u32[]{:S(2)}) collective-permute-start(f32[1024]{0:T(1024)S(1)} %collective-permute-done), channel_id=1, source_target_pairs={{0,2},{2,4},{4,6},{6,8},{8,10},{10,12},{12,14},{14,16},{16,18},{18... | collective-permute-start | bytes 12296 | tf_op jit(solution)/shard_map/ppermute | solution.py:10
  266.1 4.5 %collective-permute-start.2 = (f32[1024]{0:T(1024)S(1)}, f32[1024]{0:T(1024)S(1)}, u32[]{:S(2)}, u32[]{:S(2)}) collective-permute-start(f32[1024]{0:T(1024)S(1)} %add.119), channel_id=1, source_target_pairs={{0,4},{2,6},{4,8},{6,10},{8,12},{10,14},{12,16},{14,18},{16,20},{1... | collective-permute-start | bytes 12296 | tf_op jit(solution)/shard_map/ppermute | solution.py:10
  293.0 5.1 %collective-permute-start.4 = (f32[1024]{0:T(1024)S(1)}, f32[1024]{0:T(1024)S(1)}, u32[]{:S(2)}, u32[]{:S(2)}) collective-permute-start(f32[1024]{0:T(1024)S(1)} %add.121), channel_id=1, source_target_pairs={{0,16},{2,18},{4,20},{6,22},{8,24},{10,26},{12,28},{14,30},{1,17},... | collective-permute-start | bytes 12296 | tf_op jit(solution)/shard_map/ppermute | solution.py:10
  298.2 9.7 %fusion.96 = f32[512,1024]{1,0:T(8,128)S(1)} fusion(f32[512,1024]{1,0:T(8,128)} %fusion.95, f32[1024,1024]{1,0:T(8,128)} %all-gather.31.cloned.1.call-done), kind=kOutput, calls=%fused_computation.102 | convolution fusion | flops 6442450944 | bytes 8388608 | tf_op jit(solution)/shard_map/dot_general | solution.py:28
  319.6 6.4 %fusion.23 = f32[2,32,1024]{2,1,0:T(8,128)S(1)} fusion(f32[2,32,1024]{2,1,0:T(8,128)S(1)} %scatter-add.19, f32[1024,1024]{1,0:T(8,128)} %all-gather.17.cloned.1.call-done, f32[2,31,1024]{2,1,0:T(8,128)S(1)} %bitcast.164), kind=kOutput, calls=%fused_computation.22 | convolution fusion | flops 805371904 | bytes 4972544 | tf_op jit(solution)/shard_map/dot_general | solution.py:65
  334.4 4.3 %fusion.41 = f32[2,32,1024]{2,1,0:T(8,128)S(1)} fusion(f32[2,32,1024]{2,1,0:T(8,128)S(1)} %fusion.35, f32[1024,1024]{1,0:T(8,128)S(1)} %copy-done.10, f32[2,24,1024]{2,1,0:T(8,128)S(1)} %slice.117), kind=kOutput, calls=%fused_computation.28 | convolution fusion | flops 805371904 | bytes 4915200 | tf_op jit(solution)/shard_map/dot_general | solution.py:65
  (133 shorter events, 89.6 us)
Async XLA Ops:
  6.5 184.6 %copy-start = (f32[1024,512]{1,0:T(8,128)S(1)}, f32[1024,512]{1,0:T(8,128)}, u32[]{:S(2)}) copy-start(f32[1024,512]{1,0:T(8,128)} %param.15) | copy-start | bytes 6291460
  6.5 18.0 %all-gather.17.cloned.1.call-start = ((), (), s32[]{:S(2)}) async-start(), calls=%async_computation | async-start | bytes 6291456 | tf_op jit(solution)/shard_map/all_gather | solution.py:99
  7.3 42.5 %all-gather.19.cloned.1.call-start = ((), (), s32[]{:S(2)}) async-start(), calls=%async_computation.1 | async-start | bytes 6291456 | tf_op jit(solution)/shard_map/all_gather | solution.py:44
  34.8 40.3 %all-gather.21.cloned.1.call-start = ((), (), s32[]{:S(2)}) async-start(), calls=%async_computation.2 | async-start | bytes 6291456 | tf_op jit(solution)/shard_map/all_gather | solution.py:44
  60.1 40.3 %all-gather.23.cloned.1.call-start = ((), (), s32[]{:S(2)}) async-start(), calls=%async_computation.3 | async-start | bytes 6291456 | tf_op jit(solution)/shard_map/all_gather | solution.py:44
  85.3 40.3 %all-gather.25.cloned.1.call-start = ((), (), s32[]{:S(2)}) async-start(), calls=%async_computation.4 | async-start | bytes 6291456 | tf_op jit(solution)/shard_map/all_gather | solution.py:44
  110.6 40.3 %all-gather.27.cloned.1.call-start = ((), (), s32[]{:S(2)}) async-start(), calls=%async_computation.5 | async-start | bytes 6291456 | tf_op jit(solution)/shard_map/all_gather | solution.py:32
  135.9 56.6 %all-gather.29.cloned.1.call-start = ((), (), s32[]{:S(2)}) async-start(), calls=%async_computation.6 | async-start | bytes 6291456 | tf_op jit(solution)/shard_map/all_gather | solution.py:32
  161.2 137.0 %all-gather.31.cloned.1.call-start = ((), (), s32[]{:S(2)}) async-start(), calls=%async_computation.7 | async-start | bytes 6291456 | tf_op jit(solution)/shard_map/all_gather | solution.py:32
  202.8 6.9 %copy-start.17 = (f32[1024]{0:T(1024)S(1)}, f32[1024]{0:T(1024)}, u32[]{:S(2)}) copy-start(f32[1024]{0:T(1024)} %param.17) | copy-start | bytes 12292
  239.8 7.1 %collective-permute-start.5 = (f32[1024]{0:T(1024)S(1)}, f32[1024]{0:T(1024)S(1)}, u32[]{:S(2)}, u32[]{:S(2)}) collective-permute-start(f32[1024]{0:T(1024)S(1)} %bitcast.190), channel_id=1, source_target_pairs={{2,0},{4,2},{6,4},{8,6},{10,8},{12,10},{14,12},{16,14},{18,16},{20... | collective-permute-start | bytes 12296 | tf_op jit(solution)/shard_map/ppermute | solution.py:10
  241.9 6.9 %collective-permute-start = (f32[1024]{0:T(1024)S(1)}, f32[1024]{0:T(1024)S(1)}, u32[]{:S(2)}, u32[]{:S(2)}) collective-permute-start(f32[1024]{0:T(1024)S(1)} %bitcast.189), channel_id=1, source_target_pairs={{0,2},{2,4},{4,6},{6,8},{8,10},{10,12},{12,14},{14,16},{16,18},{18... | collective-permute-start | bytes 12296 | tf_op jit(solution)/shard_map/ppermute | solution.py:10
  246.9 7.3 %collective-permute-start.6 = (f32[1024]{0:T(1024)S(1)}, f32[1024]{0:T(1024)S(1)}, u32[]{:S(2)}, u32[]{:S(2)}) collective-permute-start(f32[1024]{0:T(1024)S(1)} %collective-permute-done.5), channel_id=1, source_target_pairs={{2,0},{4,2},{6,4},{8,6},{10,8},{12,10},{14,12},{16,14},{18,16},{20... | collective-permute-start | bytes 12296 | tf_op jit(solution)/shard_map/ppermute | solution.py:10
  248.8 13.7 %copy-start.4 = (f32[512,1024]{1,0:T(8,128)S(1)}, f32[512,1024]{1,0:T(8,128)}, u32[]{:S(2)}) copy-start(f32[512,1024]{1,0:T(8,128)} %fusion.93) | copy-start | bytes 6291460
  248.8 13.6 %collective-permute-start.1 = (f32[1024]{0:T(1024)S(1)}, f32[1024]{0:T(1024)S(1)}, u32[]{:S(2)}, u32[]{:S(2)}) collective-permute-start(f32[1024]{0:T(1024)S(1)} %collective-permute-done), channel_id=1, source_target_pairs={{0,2},{2,4},{4,6},{6,8},{8,10},{10,12},{12,14},{14,16},{16,18},{18... | collective-permute-start | bytes 12296 | tf_op jit(solution)/shard_map/ppermute | solution.py:10
  254.1 16.6 %copy-start.3 = (f32[512,1024]{1,0:T(8,128)S(1)}, f32[512,1024]{1,0:T(8,128)}, u32[]{:S(2)}) copy-start(f32[512,1024]{1,0:T(8,128)} %fusion.94) | copy-start | bytes 6291460
  260.5 10.1 %collective-permute-start.7 = (f32[1024]{0:T(1024)S(1)}, f32[1024]{0:T(1024)S(1)}, u32[]{:S(2)}, u32[]{:S(2)}) collective-permute-start(f32[1024]{0:T(1024)S(1)} %add.124), channel_id=1, source_target_pairs={{4,0},{6,2},{8,4},{10,6},{12,8},{14,10},{16,12},{18,14},{20,16},{2... | collective-permute-start | bytes 12296 | tf_op jit(solution)/shard_map/ppermute | solution.py:10
  266.1 9.8 %collective-permute-start.2 = (f32[1024]{0:T(1024)S(1)}, f32[1024]{0:T(1024)S(1)}, u32[]{:S(2)}, u32[]{:S(2)}) collective-permute-start(f32[1024]{0:T(1024)S(1)} %add.119), channel_id=1, source_target_pairs={{0,4},{2,6},{4,8},{6,10},{8,12},{10,14},{12,16},{14,18},{16,20},{1... | collective-permute-start | bytes 12296 | tf_op jit(solution)/shard_map/ppermute | solution.py:10
  270.7 13.2 %copy-start.2 = (f32[512,1024]{1,0:T(8,128)S(1)}, f32[512,1024]{1,0:T(8,128)}, u32[]{:S(2)}) copy-start(f32[512,1024]{1,0:T(8,128)} %fusion.95) | copy-start | bytes 6291460
  274.6 9.2 %collective-permute-start.8 = (f32[1024]{0:T(1024)S(1)}, f32[1024]{0:T(1024)S(1)}, u32[]{:S(2)}, u32[]{:S(2)}) collective-permute-start(f32[1024]{0:T(1024)S(1)} %add.125), channel_id=1, source_target_pairs={{8,0},{10,2},{12,4},{14,6},{16,8},{18,10},{20,12},{22,14},{24,16},... | collective-permute-start | bytes 12296 | tf_op jit(solution)/shard_map/ppermute | solution.py:10
  279.6 9.7 %collective-permute-start.3 = (f32[1024]{0:T(1024)S(1)}, f32[1024]{0:T(1024)S(1)}, u32[]{:S(2)}, u32[]{:S(2)}) collective-permute-start(f32[1024]{0:T(1024)S(1)} %add.120), channel_id=1, source_target_pairs={{0,8},{2,10},{4,12},{6,14},{8,16},{10,18},{12,20},{14,22},{16,24},... | collective-permute-start | bytes 12296 | tf_op jit(solution)/shard_map/ppermute | solution.py:10
  287.8 20.0 %collective-permute-start.9 = (f32[1024]{0:T(1024)S(1)}, f32[1024]{0:T(1024)S(1)}, u32[]{:S(2)}, u32[]{:S(2)}) collective-permute-start(f32[1024]{0:T(1024)S(1)} %add.126), channel_id=1, source_target_pairs={{16,0},{18,2},{20,4},{22,6},{24,8},{26,10},{28,12},{30,14},{17,1},... | collective-permute-start | bytes 12296 | tf_op jit(solution)/shard_map/ppermute | solution.py:10
  293.0 18.8 %collective-permute-start.4 = (f32[1024]{0:T(1024)S(1)}, f32[1024]{0:T(1024)S(1)}, u32[]{:S(2)}, u32[]{:S(2)}) collective-permute-start(f32[1024]{0:T(1024)S(1)} %add.121), channel_id=1, source_target_pairs={{0,16},{2,18},{4,20},{6,22},{8,24},{10,26},{12,28},{14,30},{1,17},... | collective-permute-start | bytes 12296 | tf_op jit(solution)/shard_map/ppermute | solution.py:10
  307.9 7.6 %copy-start.1 = (f32[1024,1024]{1,0:T(8,128)S(1)}, f32[1024,1024]{1,0:T(8,128)}, u32[]{:S(2)}) copy-start(f32[1024,1024]{1,0:T(8,128)} %all-gather.17.cloned.1.call-done) | copy-start | bytes 12582916
  (14 other events, 49.1 us)
Sparse Core Ops, SparseCore 0:
  8.9 15.5 all-gather.16
  34.9 14.8 all-gather.18
  60.2 14.8 all-gather.20
  85.5 14.8 all-gather.22
  110.7 14.8 all-gather.24
  136.0 14.8 all-gather.26
  161.4 14.8 all-gather.28
  202.9 14.8 all-gather.30
where the time goes:
time: 361 us; the launch traced here: 354 us
  matrix products  162 us (45%)
  waiting for transfers between devices  92.7 us (26%)
  starting transfers between devices  33.4 us (9%)
  other arithmetic  29.3 us (8%)
  blocking collectives  20 us (6%)
  between operations  14.3 us (4%)
    dot_general x8, matrix products, accumulate(): return jnp.dot(slab_rows, block_rows, precision=lax.Precision.HIGHEST)  81.5 us
    all_gather x4, waiting for transfers between devices, ladder_slabs(): full_list.append(lax.all_gather(squared, 'row', axis=0, tiled=True))  59.6 us
    dot_general x10, matrix products, sweep(): lax.dot_general(shifted, power, (((2,), (1,)), ((), ())), precision=lax.P...  46.2 us
    ppermute x10, starting transfers between devices, passed_along(): return lax.ppermute(array, axis, pairs)  32.9 us
    unnamed x4, other arithmetic  29.1 us
    all_gather x1, waiting for transfers between devices, per_device(): full_matrix = lax.all_gather(transition, 'row', axis=0, tiled=True)  17.2 us
    all_gather x3, waiting for transfers between devices, square_level(): lax.all_gather(slab_rows, 'row', axis=0, tiled=True)  15 us
    dot_general x2, matrix products, sweep(): lax.dot_general(starts, full_list[0], contract, precision=lax.Precision.H...  9.75 us
  transfers between devices with their start and end apart: 18, of which 6 were waited for; matrix products, arithmetic and copies ran while one was open for 25% of the time, Pallas kernels for 0%

commit v1 on v0

v1 whole, which is shorter than its diff:
```python
import functools

import jax
import jax.numpy as jnp
from jax import lax
from jax.experimental import pallas as pl
from jax.experimental.pallas import tpu as pltpu
from jax.sharding import PartitionSpec as P

MESH = pl.DeviceIdType.MESH
F32, BF16 = jnp.float32, jnp.bfloat16
LANES = 128


def halves(x):
    high = x.astype(BF16)
    return high, (x - high.astype(F32)).astype(BF16)


def dot(a, b):
    return jnp.dot(a, b, preferred_element_type=F32)


def product(x, w_high, w_low):
    rows = x.shape[0]
    high, low = halves(x)
    both = dot(jnp.concatenate([high, low], axis=0), w_high)
    return both[:rows] + both[rows:] + dot(high, w_low)


def as_rows(ref):
    return jnp.concatenate([ref[:, i, :] for i in range(ref.shape[1])], axis=1)


def kernel(
    segments, levels, tile,
    a_hbm, gf_hbm, gb_hbm, bl_hbm, ends_ref, index_ref, visible_ref, value_ref,
    out_ref,
    a_full, gains, blend, blend_high, blend_low, high, low, sparse, fg, v_in, v_ref,
    f_send, f_all, paths, in_sem, a_send, a_recv, v_send, v_recv, f_send_sem, f_recv_sem,
    x_send, x_recv,
):
    seg = lax.axis_index("tm")
    row = lax.axis_index("row")
    other = 1 - row
    half, size = a_hbm.shape
    epochs = index_ref.shape[0]
    place = seg + row * (segments - 1 - 2 * seg)

    gf_copy = pltpu.make_async_copy(gf_hbm, gains.at[0], in_sem.at[0])
    gb_copy = pltpu.make_async_copy(gb_hbm, gains.at[1], in_sem.at[1])
    bl_copy = pltpu.make_async_copy(bl_hbm, blend, in_sem.at[2])
    own_copy = pltpu.make_async_copy(a_hbm, a_full.at[row], in_sem.at[3])

    barrier = pltpu.get_barrier_semaphore()
    pl.semaphore_signal(barrier, inc=1, device_id=(seg, other), device_id_type=MESH)

    def greet(d, carry):
        pl.semaphore_signal(
            barrier, inc=1, device_id=(lax.rem(seg + d, segments), row), device_id_type=MESH
        )
        return carry

    lax.fori_loop(1, segments, greet, 0)
    gf_copy.start()
    gb_copy.start()
    own_copy.start()
    bl_copy.start()
    pl.semaphore_wait(barrier, segments)

    a_copy = pltpu.make_async_remote_copy(
        src_ref=a_hbm, dst_ref=a_full.at[row], send_sem=a_send, recv_sem=a_recv,
        device_id=(seg, other), device_id_type=MESH,
    )
    a_copy.start()

    groups = size // LANES
    slots = index_ref.shape[1]
    weights = value_ref[...] * visible_ref[...].astype(F32)
    index = index_ref[...]
    group, lane = index // LANES, index % LANES
    group_iota = lax.broadcasted_iota(jnp.int32, (groups, slots), 0)
    lane_iota = lax.broadcasted_iota(jnp.int32, (LANES, slots), 0)
    for k in range(epochs):
        left = jnp.where(group[k : k + 1, :] == group_iota, weights[k : k + 1, :], 0.0)
        right = jnp.where(lane[k : k + 1, :] == lane_iota, 1.0, 0.0).astype(BF16)
        top, mid = halves(left)
        rest = (left - top.astype(F32) - mid.astype(F32)).astype(BF16)
        sums = lax.dot_general(
            jnp.concatenate([top, mid, rest], axis=0), right, (((1,), (1,)), ((), ())),
            preferred_element_type=F32,
        )
        sums = sums[:groups] + sums[groups : 2 * groups] + sums[2 * groups :]
        sparse[0, k] = sums
        sparse[1, epochs - 1 - k] = sums

    gf_copy.wait()
    gb_copy.wait()
    for way in range(2):
        gain_high, gain_low = halves(gains[way])
        fg[way] = product(as_rows(sparse.at[way]), gain_high, gain_low)
    v_copy = pltpu.make_async_remote_copy(
        src_ref=fg.at[other], dst_ref=v_in.at[row], send_sem=v_send, recv_sem=v_recv,
        device_id=(seg, other), device_id_type=MESH,
    )
    v_copy.start()
    v_in[row] = fg[row]

    bl_copy.wait()
    bl_high, bl_low = halves(blend[...])
    blend_high[...] = bl_high
    blend_low[...] = bl_low

    own_copy.wait()
    a_copy.wait_recv()
    for part in range(2):
        diagonal = lax.broadcasted_iota(jnp.int32, (half, size), 1) == (
            lax.broadcasted_iota(jnp.int32, (half, size), 0) + part * half
        )
        first = jnp.where(diagonal, 1.0, 0.0) - a_full[part]
        first_high, first_low = halves(first)
        high[0, part * half : (part + 1) * half, :] = first_high
        low[0, part * half : (part + 1) * half, :] = first_low

    v_copy.wait_recv()
    v_ref[...] = jnp.concatenate([v_in[0], v_in[1]], axis=1)
    epoch_iota = lax.broadcasted_iota(jnp.int32, (epochs, size), 0)

    def send_all(d):
        target = lax.rem(seg + d, segments)
        return pltpu.make_async_remote_copy(
            src_ref=f_send, dst_ref=f_all.at[place + 1],
            send_sem=f_send_sem.at[d], recv_sem=f_recv_sem.at[d],
            device_id=(target, row), device_id_type=MESH,
        )

    def level_step(level, carry):
        step = lax.shift_left(jnp.int32(1), level)
        now = v_ref[...]
        shifted = jnp.where(epoch_iota >= step, pltpu.roll(now, step, 0), 0.0)
        v_ref[...] = now + shifted - product(shifted, high[level], low[level])

        @pl.when(level == levels - 1)
        def _():
            for i in range(groups):
                f_send[i : i + 1, :] = v_ref[epochs - 1 : epochs, i * LANES : (i + 1) * LANES]

            def start(d, c):
                send_all(d).start()
                return c

            lax.fori_loop(1, segments, start, 0)

        for j in range(size // tile):
            columns = slice(j * tile, (j + 1) * tile)
            right_high = high[level, :, columns]
            right_low = low[level, :, columns]
            for i in range(j + 1):
                rows = slice(i * tile, (i + 1) * tile)
                left_high = high[level, rows, :]
                square = (
                    dot(left_high, right_high)
                    + dot(low[level, rows, :], right_high)
                    + dot(left_high, right_low)
                )
                block = high[level, rows, columns].astype(F32) + low[level, rows, columns].astype(F32)
                block = 2.0 * block - square
                block_high, block_low = halves(block)
                high[level + 1, rows, columns] = block_high
                low[level + 1, rows, columns] = block_low
                if i < j:
                    high[level + 1, columns, rows] = block_high.T
                    low[level + 1, columns, rows] = block_low.T
        return carry

    lax.fori_loop(0, levels, level_step, 0)

    def finish(d, carry):
        copy = send_all(d)
        copy.wait_recv()
        copy.wait_send()
        return carry

    lax.fori_loop(1, segments, finish, 0)
    f_all[place + 1] = f_send[...]
    first_state = jnp.where(row == 0, ends_ref[0:1, :], ends_ref[1:2, :])
    for i in range(groups):
        f_all[0, i : i + 1, :] = first_state[:, i * LANES : (i + 1) * LANES]

    def entry(j):
        block = f_all[j]
        return jnp.broadcast_to(
            jnp.concatenate([block[i : i + 1, :] for i in range(groups)], axis=1), (8, size)
        )

    def advance(j, state):
        return state - product(state, high[levels], low[levels]) + entry(j)

    start = lax.fori_loop(1, place + 1, advance, entry(0))

    def spread(level, state):
        chosen = lax.rem(lax.shift_right_logical(epoch_iota + 1, level), 2) == 1
        return jnp.where(chosen, state - product(state, high[level], low[level]), state)

    spread_start = jnp.concatenate([start] * (epochs // 8), axis=0)
    v_ref[...] += lax.fori_loop(0, levels + 1, spread, spread_start)

    for k in range(epochs):
        back = epochs - 1 - k
        paths[row, k : k + 1, :] = jnp.where(row == 0, v_ref[k : k + 1, :], v_ref[back : back + 1, :])
    x_copy = pltpu.make_async_remote_copy(
        src_ref=paths.at[row], dst_ref=paths.at[row], send_sem=x_send, recv_sem=x_recv,
        device_id=(seg, other), device_id_type=MESH,
    )
    x_copy.start()
    own = product(paths[row], blend_high[...], blend_low[...])
    x_copy.wait_recv()
    theirs = product(paths[other], blend_high[...], blend_low[...])
    gap = own - theirs
    mine = paths[0, :, pl.ds(pl.multiple_of(row * half, LANES), half)]
    out_ref[...] = mine + jnp.where(row == 1, gap, -gap)
    x_copy.wait_send()
    v_copy.wait_send()
    a_copy.wait_send()


def per_device(
    segments, transition, gain_fwd, gain_bwd, blend, prior_state, final_state,
    obs_index, obs_visible, obs_value,
):
    half, size = transition.shape
    epochs = obs_index.shape[0]
    levels = (epochs - 1).bit_length()
    groups = size // LANES
    ends = jnp.stack([prior_state, final_state], axis=0)
    anywhere = pl.BlockSpec(memory_space=pl.ANY)
    vmem = pl.BlockSpec(memory_space=pltpu.VMEM)
    dma = pltpu.SemaphoreType.DMA
    return pl.pallas_call(
        functools.partial(kernel, segments, levels, min(256, size)),
        out_shape=jax.ShapeDtypeStruct((epochs, half), F32),
        in_specs=[anywhere] * 4 + [vmem] * 4,
        out_specs=vmem,
        scratch_shapes=[
            pltpu.VMEM((2, half, size), F32),
            pltpu.VMEM((2, size, half), F32),
            pltpu.VMEM((size, half), F32),
            pltpu.VMEM((size, half), BF16),
            pltpu.VMEM((size, half), BF16),
            pltpu.VMEM((levels + 1, size, size), BF16),
            pltpu.VMEM((levels + 1, size, size), BF16),
            pltpu.VMEM((2, epochs, groups, LANES), F32),
            pltpu.VMEM((2, epochs, half), F32),
            pltpu.VMEM((2, epochs, half), F32),
            pltpu.VMEM((epochs, size), F32),
            pltpu.VMEM((groups, LANES), F32),
            pltpu.VMEM((segments + 1, groups, LANES), F32),
            pltpu.VMEM((2, epochs, size), F32),
            dma((4,)), dma, dma, dma, dma, dma((segments,)), dma((segments,)), dma, dma,
        ],
        compiler_params=pltpu.CompilerParams(
            collective_id=0, has_side_effects=True, vmem_limit_bytes=60 * 2**20
        ),
    )(transition, gain_fwd, gain_bwd, blend, ends, obs_index, obs_visible, obs_value)


def solution(mesh):
    placed = (
        P("row", None), P(None, "row"), P(None, "row"), P(None, "row"), P(), P(),
        P("tm", None), P("tm", None), P("tm", None),
    )
    return jax.shard_map(
        functools.partial(per_device, mesh.shape["tm"]),
        mesh=mesh, in_specs=placed, out_specs=P("tm", "row"), check_vma=False,
    )
```

time: 361 us -> 60.6 us (0.17)
  the two profiles are of different devices: /device:TPU:7 before, /device:TPU:0 now
where the time goes in v1:
time: 60.6 us; the launch traced here: 60.3 us
  Pallas kernels  57.5 us (95%)
  local copies, waits for them, and re-layouts  1.47 us (2%)
  other arithmetic  1.31 us (2%)
    pallas_call x1, Pallas kernels, per_device(): pl.pallas_call(functools.partial(kernel, segments, levels, min(256, size)...  57.5 us
    unnamed x1, local copies, waits for them, and re-layouts  1.47 us
    another operation x1, other arithmetic, per_device(): ends = jnp.stack([prior_state, final_state], axis=0)  1.31 us

profile of v1, /device:TPU:0, one launch (start us, length us, event | category | flops | bytes accessed | tf_op | source)
XLA Modules:
  0.0 60.3 jit_solution(6489530764096886718)
XLA Ops:
  0.0 1.3 %pad_maximum_fusion.ends_ref = f32[2,1024]{1,0:T(2,128)} fusion(f32[1,1024]{1,0:T(1,128)} %bitcast.2, f32[1,1024]{1,0:T(1,128)} %bitcast.3), kind=kLoop, calls=%fused_computation | loop fusion | flops 2048 | bytes 16384 | tf_op jit(solution)/shard_map/stack | solution.py:235
  1.3 57.5 %shard_map.91 = f32[32,512]{1,0:T(8,128)} custom-call(f32[512,1024]{1,0:T(8,128)} %a_hbm.1, f32[1024,512]{1,0:T(8,128)} %gf_hbm.1, f32[1024,512]{1,0:T(8,128)} %gb_hbm.1, f32[1024,512]{1,0:T(8,128)} %bl_hbm.1, f32[2,1024]{1,0:T(2,128)} %pad_maximum_fusion.ends_ref, s32[32,128]{1,0:T(8,128)} %index_ref.1, s32[32,128]{1,0:T(8,128)} %visible_ref.1, ...), custom_call_target="tpu_custom_call" | custom-call | tf_op jit(solution)/shard_map/pallas_call | solution.py:239
  58.8 1.5 %copy.11 = f32[32,512]{1,0:T(8,128)} copy(f32[32,512]{1,0:T(8,128)} %shard_map.91) | data formatting | bytes 131072

commit v2 on v1

--- a/solution.py
+++ b/solution.py
@@ -36,7 +36,7 @@
     segments, levels, tile,
     a_hbm, gf_hbm, gb_hbm, bl_hbm, ends_ref, index_ref, visible_ref, value_ref,
     out_ref,
-    a_full, gains, blend, blend_high, blend_low, high, low, sparse, fg, v_in, v_ref,
+    a_own, a_other, a_map, gains, blend, blend_high, blend_low, high, low, sparse, fg, v_in, v_ref,
     f_send, f_all, paths, in_sem, a_send, a_recv, v_send, v_recv, f_send_sem, f_recv_sem,
     x_send, x_recv,
 ):
@@ -50,7 +50,7 @@
     gf_copy = pltpu.make_async_copy(gf_hbm, gains.at[0], in_sem.at[0])
     gb_copy = pltpu.make_async_copy(gb_hbm, gains.at[1], in_sem.at[1])
     bl_copy = pltpu.make_async_copy(bl_hbm, blend, in_sem.at[2])
-    own_copy = pltpu.make_async_copy(a_hbm, a_full.at[row], in_sem.at[3])
+    own_copy = pltpu.make_async_copy(a_hbm, a_own, in_sem.at[3])
 
     barrier = pltpu.get_barrier_semaphore()
     pl.semaphore_signal(barrier, inc=1, device_id=(seg, other), device_id_type=MESH)
@@ -68,11 +68,21 @@
     bl_copy.start()
     pl.semaphore_wait(barrier, segments)
 
-    a_copy = pltpu.make_async_remote_copy(
-        src_ref=a_hbm, dst_ref=a_full.at[row], send_sem=a_send, recv_sem=a_recv,
-        device_id=(seg, other), device_id_type=MESH,
-    )
-    a_copy.start()
+    own_part = pl.ds(pl.multiple_of(row * half, half), half)
+    other_part = pl.ds(pl.multiple_of(other * half, half), half)
+    pieces = a_send.shape[0]
+    piece = half // pieces
+    a_copies = [
+        pltpu.make_async_remote_copy(
+            src_ref=a_hbm.at[pl.ds(c * piece, piece), own_part],
+            dst_ref=a_other.at[pl.ds(c * piece, piece), :],
+            send_sem=a_send.at[c], recv_sem=a_recv.at[c],
+            device_id=(seg, other), device_id_type=MESH,
+        )
+        for c in range(pieces)
+    ]
+    for copy in a_copies:
+        copy.start()
 
     groups = size // LANES
     slots = index_ref.shape[1]
@@ -112,15 +122,23 @@
     blend_low[...] = bl_low
 
     own_copy.wait()
-    a_copy.wait_recv()
-    for part in range(2):
-        diagonal = lax.broadcasted_iota(jnp.int32, (half, size), 1) == (
-            lax.broadcasted_iota(jnp.int32, (half, size), 0) + part * half
-        )
-        first = jnp.where(diagonal, 1.0, 0.0) - a_full[part]
-        first_high, first_low = halves(first)
-        high[0, part * half : (part + 1) * half, :] = first_high
-        low[0, part * half : (part + 1) * half, :] = first_low
+    identity = jnp.where(
+        lax.broadcasted_iota(jnp.int32, (half, half), 0)
+        == lax.broadcasted_iota(jnp.int32, (half, half), 1), 1.0, 0.0,
+    )
+    block_high, block_low = halves(identity - a_own[:, own_part])
+    high[0, own_part, own_part] = block_high
+    low[0, own_part, own_part] = block_low
+    block_high, block_low = halves(-a_own[:, other_part])
+    high[0, own_part, other_part] = block_high
+    low[0, own_part, other_part] = block_low
+    high[0, other_part, own_part] = block_high.T
+    low[0, other_part, own_part] = block_low.T
+    for copy in a_copies:
+        copy.wait_recv()
+    block_high, block_low = halves(identity - a_other[...])
+    high[0, other_part, other_part] = block_high
+    low[0, other_part, other_part] = block_low
 
     v_copy.wait_recv()
     v_ref[...] = jnp.concatenate([v_in[0], v_in[1]], axis=1)
@@ -151,29 +169,40 @@
 
             lax.fori_loop(1, segments, start, 0)
 
-        for j in range(size // tile):
-            columns = slice(j * tile, (j + 1) * tile)
-            right_high = high[level, :, columns]
-            right_low = low[level, :, columns]
-            for i in range(j + 1):
-                rows = slice(i * tile, (i + 1) * tile)
-                left_high = high[level, rows, :]
+        @pl.when(level < levels - 1)
+        def _():
+            for j in range(size // tile):
+                columns = slice(j * tile, (j + 1) * tile)
+                right_high = high[level, :, columns]
+                right_low = low[level, :, columns]
+                upper = slice(0, (j + 1) * tile)
+                left_high = high[level, upper, :]
                 square = (
                     dot(left_high, right_high)
-                    + dot(low[level, rows, :], right_high)
+                    + dot(low[level, upper, :], right_high)
                     + dot(left_high, right_low)
                 )
-                block = high[level, rows, columns].astype(F32) + low[level, rows, columns].astype(F32)
+                block = high[level, upper, columns].astype(F32) + low[level, upper, columns].astype(F32)
                 block = 2.0 * block - square
                 block_high, block_low = halves(block)
-                high[level + 1, rows, columns] = block_high
-                low[level + 1, rows, columns] = block_low
-                if i < j:
-                    high[level + 1, columns, rows] = block_high.T
-                    low[level + 1, columns, rows] = block_low.T
+                high[level + 1, upper, columns] = block_high
+                low[level + 1, upper, columns] = block_low
+                if j > 0:
+                    high[level + 1, columns, : j * tile] = block_high[: j * tile].T
+                    low[level + 1, columns, : j * tile] = block_low[: j * tile].T
+
         return carry
 
     lax.fori_loop(0, levels, level_step, 0)
+
+    for i in range(size // tile):
+        rows = slice(i * tile, (i + 1) * tile)
+        diagonal = lax.broadcasted_iota(jnp.int32, (tile, size), 1) == (
+            lax.broadcasted_iota(jnp.int32, (tile, size), 0) + i * tile
+        )
+        a_map[rows, :] = (
+            jnp.where(diagonal, 1.0, 0.0) - high[levels - 1, rows, :].astype(F32)
+        ) - low[levels - 1, rows, :].astype(F32)
 
     def finish(d, carry):
         copy = send_all(d)
@@ -193,14 +222,28 @@
             jnp.concatenate([block[i : i + 1, :] for i in range(groups)], axis=1), (8, size)
         )
 
+    chunk = 32
+
     def advance(j, state):
-        return state - product(state, high[levels], low[levels]) + entry(j)
+        total = jnp.zeros((8, size), F32)
+        for i in range(size // chunk):
+            rows = a_map[i * chunk : (i + 1) * chunk, :]
+            dots = jnp.sum(
+                (rows.reshape(chunk // 8, 8, size) * state[None]).reshape(chunk, size),
+                axis=1, keepdims=True,
+            )
+            total = total + jnp.sum((rows * dots).reshape(chunk // 8, 8, size), axis=0)
+        return jnp.broadcast_to(jnp.sum(total, axis=0, keepdims=True), (8, size)) + entry(j)
 
     start = lax.fori_loop(1, place + 1, advance, entry(0))
 
+    turns = epoch_iota + 1
+    turns = jnp.where(turns == epochs, epochs + epochs // 2, turns)
+
     def spread(level, state):
-        chosen = lax.rem(lax.shift_right_logical(epoch_iota + 1, level), 2) == 1
-        return jnp.where(chosen, state - product(state, high[level], low[level]), state)
+        power = jnp.minimum(level, levels - 1)
+        chosen = lax.rem(lax.shift_right_logical(turns, level), 2) == 1
+        return jnp.where(chosen, state - product(state, high[power], low[power]), state)
 
     spread_start = jnp.concatenate([start] * (epochs // 8), axis=0)
     v_ref[...] += lax.fori_loop(0, levels + 1, spread, spread_start)
@@ -221,7 +264,8 @@
     out_ref[...] = mine + jnp.where(row == 1, gap, -gap)
     x_copy.wait_send()
     v_copy.wait_send()
-    a_copy.wait_send()
+    for copy in a_copies:
+        copy.wait_send()
 
 
 def per_device(
@@ -242,13 +286,15 @@
         in_specs=[anywhere] * 4 + [vmem] * 4,
         out_specs=vmem,
         scratch_shapes=[
-            pltpu.VMEM((2, half, size), F32),
+            pltpu.VMEM((half, size), F32),
+            pltpu.VMEM((half, half), F32),
+            pltpu.VMEM((size, size), F32),
             pltpu.VMEM((2, size, half), F32),
             pltpu.VMEM((size, half), F32),
             pltpu.VMEM((size, half), BF16),
             pltpu.VMEM((size, half), BF16),
-            pltpu.VMEM((levels + 1, size, size), BF16),
-            pltpu.VMEM((levels + 1, size, size), BF16),
+            pltpu.VMEM((levels, size, size), BF16),
+            pltpu.VMEM((levels, size, size), BF16),
             pltpu.VMEM((2, epochs, groups, LANES), F32),
             pltpu.VMEM((2, epochs, half), F32),
             pltpu.VMEM((2, epochs, half), F32),
@@ -256,7 +302,7 @@
             pltpu.VMEM((groups, LANES), F32),
             pltpu.VMEM((segments + 1, groups, LANES), F32),
             pltpu.VMEM((2, epochs, size), F32),
-            dma((4,)), dma, dma, dma, dma, dma((segments,)), dma((segments,)), dma, dma,
+            dma((4,)), dma((4,)), dma((4,)), dma, dma, dma((segments,)), dma((segments,)), dma, dma,
         ],
         compiler_params=pltpu.CompilerParams(
             collective_id=0, has_side_effects=True, vmem_limit_bytes=60 * 2**20

time: 60.6 us -> 53.6 us (0.88)
  Pallas kernels: 57.5 us -> 50.4 us
    pallas_call x1, Pallas kernels: 57.5 us -> 50.4 us  [per_device(): pl.pallas_call(functools.partial(kernel, segments, levels, min(256, size)...]
where the time goes in v2:
time: 53.6 us; the launch traced here: 53.2 us
  Pallas kernels  50.4 us (94%)
  local copies, waits for them, and re-layouts  1.47 us (3%)
  other arithmetic  1.31 us (2%)
    pallas_call x1, Pallas kernels, per_device(): pl.pallas_call(functools.partial(kernel, segments, levels, min(256, size)...  50.4 us
    unnamed x1, local copies, waits for them, and re-layouts  1.47 us
    another operation x1, other arithmetic, per_device(): ends = jnp.stack([prior_state, final_state], axis=0)  1.31 us

profile of v2, /device:TPU:0, one launch (start us, length us, event | category | flops | bytes accessed | tf_op | source)
XLA Modules:
  0.0 53.2 jit_solution(17346846614350814321)
XLA Ops:
  0.0 1.3 %pad_maximum_fusion.ends_ref = f32[2,1024]{1,0:T(2,128)} fusion(f32[1,1024]{1,0:T(1,128)} %bitcast.2, f32[1,1024]{1,0:T(1,128)} %bitcast.3), kind=kLoop, calls=%fused_computation | loop fusion | flops 2048 | bytes 16384 | tf_op jit(solution)/shard_map/stack | solution.py:279
  1.3 50.4 %shard_map.91 = f32[32,512]{1,0:T(8,128)} custom-call(f32[512,1024]{1,0:T(8,128)} %a_hbm.1, f32[1024,512]{1,0:T(8,128)} %gf_hbm.1, f32[1024,512]{1,0:T(8,128)} %gb_hbm.1, f32[1024,512]{1,0:T(8,128)} %bl_hbm.1, f32[2,1024]{1,0:T(2,128)} %pad_maximum_fusion.ends_ref, s32[32,128]{1,0:T(8,128)} %index_ref.1, s32[32,128]{1,0:T(8,128)} %visible_ref.1, ...), custom_call_target="tpu_custom_call" | custom-call | tf_op jit(solution)/shard_map/pallas_call | solution.py:283
  51.7 1.5 %copy.11 = f32[32,512]{1,0:T(8,128)} copy(f32[32,512]{1,0:T(8,128)} %shard_map.91) | data formatting | bytes 131072

commit v3 on v2

--- a/solution.py
+++ b/solution.py
@@ -156,10 +156,11 @@
         step = lax.shift_left(jnp.int32(1), level)
         now = v_ref[...]
         shifted = jnp.where(epoch_iota >= step, pltpu.roll(now, step, 0), 0.0)
-        v_ref[...] = now + shifted - product(shifted, high[level], low[level])
+        shift_high, shift_low = halves(shifted)
 
         @pl.when(level == levels - 1)
         def _():
+            v_ref[...] = now + shifted - product(shifted, high[level], low[level])
             for i in range(groups):
                 f_send[i : i + 1, :] = v_ref[epochs - 1 : epochs, i * LANES : (i + 1) * LANES]
 
@@ -177,11 +178,12 @@
                 right_low = low[level, :, columns]
                 upper = slice(0, (j + 1) * tile)
                 left_high = high[level, upper, :]
-                square = (
-                    dot(left_high, right_high)
-                    + dot(low[level, upper, :], right_high)
-                    + dot(left_high, right_low)
+                by_high = dot(jnp.concatenate([shift_high, shift_low, left_high], axis=0), right_high)
+                by_low = dot(jnp.concatenate([shift_high, left_high], axis=0), right_low)
+                v_ref[:, columns] = (now[:, columns] + shifted[:, columns]) - (
+                    by_high[:epochs] + by_high[epochs : 2 * epochs] + by_low[:epochs]
                 )
+                square = by_high[2 * epochs :] + dot(low[level, upper, :], right_high) + by_low[epochs:]
                 block = high[level, upper, columns].astype(F32) + low[level, upper, columns].astype(F32)
                 block = 2.0 * block - square
                 block_high, block_low = halves(block)
@@ -224,7 +226,7 @@
 
     chunk = 32
 
-    def advance(j, state):
+    def two_steps(state):
         total = jnp.zeros((8, size), F32)
         for i in range(size // chunk):
             rows = a_map[i * chunk : (i + 1) * chunk, :]
@@ -233,20 +235,21 @@
                 axis=1, keepdims=True,
             )
             total = total + jnp.sum((rows * dots).reshape(chunk // 8, 8, size), axis=0)
-        return jnp.broadcast_to(jnp.sum(total, axis=0, keepdims=True), (8, size)) + entry(j)
+        return jnp.broadcast_to(jnp.sum(total, axis=0, keepdims=True), (8, size))
+
+    def advance(j, state):
+        return two_steps(state) + entry(j)
 
     start = lax.fori_loop(1, place + 1, advance, entry(0))
 
-    turns = epoch_iota + 1
-    turns = jnp.where(turns == epochs, epochs + epochs // 2, turns)
-
     def spread(level, state):
-        power = jnp.minimum(level, levels - 1)
-        chosen = lax.rem(lax.shift_right_logical(turns, level), 2) == 1
-        return jnp.where(chosen, state - product(state, high[power], low[power]), state)
+        chosen = lax.rem(lax.shift_right_logical(epoch_iota + 1, level), 2) == 1
+        return jnp.where(chosen, state - product(state, high[level], low[level]), state)
 
     spread_start = jnp.concatenate([start] * (epochs // 8), axis=0)
-    v_ref[...] += lax.fori_loop(0, levels + 1, spread, spread_start)
+    through = jnp.concatenate([two_steps(start)] * (epochs // 8), axis=0)
+    within = lax.fori_loop(0, levels, spread, spread_start)
+    v_ref[...] += jnp.where(epoch_iota == epochs - 1, through, within)
 
     for k in range(epochs):
         back = epochs - 1 - k

time: 53.6 us -> 51.5 us (0.961)
  Pallas kernels: 50.4 us -> 48.3 us
    pallas_call x1, Pallas kernels: 50.4 us -> 48.3 us  [per_device(): pl.pallas_call(functools.partial(kernel, segments, levels, min(256, size)...]
where the time goes in v3:
time: 51.5 us; the launch traced here: 51.1 us
  Pallas kernels  48.3 us (94%)
  local copies, waits for them, and re-layouts  1.47 us (3%)
  other arithmetic  1.31 us (3%)
    pallas_call x1, Pallas kernels, per_device(): pl.pallas_call(functools.partial(kernel, segments, levels, min(256, size)...  48.3 us
    unnamed x1, local copies, waits for them, and re-layouts  1.47 us
    another operation x1, other arithmetic, per_device(): ends = jnp.stack([prior_state, final_state], axis=0)  1.31 us

profile of v3, /device:TPU:0, one launch (start us, length us, event | category | flops | bytes accessed | tf_op | source)
XLA Modules:
  0.0 51.1 jit_solution(3071062922869440475)
XLA Ops:
  0.0 1.3 %pad_maximum_fusion.ends_ref = f32[2,1024]{1,0:T(2,128)} fusion(f32[1,1024]{1,0:T(1,128)} %bitcast.2, f32[1,1024]{1,0:T(1,128)} %bitcast.3), kind=kLoop, calls=%fused_computation | loop fusion | flops 2048 | bytes 16384 | tf_op jit(solution)/shard_map/stack | solution.py:282
  1.3 48.3 %shard_map.91 = f32[32,512]{1,0:T(8,128)} custom-call(f32[512,1024]{1,0:T(8,128)} %a_hbm.1, f32[1024,512]{1,0:T(8,128)} %gf_hbm.1, f32[1024,512]{1,0:T(8,128)} %gb_hbm.1, f32[1024,512]{1,0:T(8,128)} %bl_hbm.1, f32[2,1024]{1,0:T(2,128)} %pad_maximum_fusion.ends_ref, s32[32,128]{1,0:T(8,128)} %index_ref.1, s32[32,128]{1,0:T(8,128)} %visible_ref.1, ...), custom_call_target="tpu_custom_call" | custom-call | tf_op jit(solution)/shard_map/pallas_call | solution.py:286
  49.6 1.5 %copy.11 = f32[32,512]{1,0:T(8,128)} copy(f32[32,512]{1,0:T(8,128)} %shard_map.91) | data formatting | bytes 131072
